TPU v7x, 32 devices: a whole 2x2x4 slice. The times are simulated.
32 devices in a mesh: lon: 8 (over z, y), lat: 4 (over x, core).
Axes of the slice: x: 2, y: 2, z: 4, core: 2. Of those that a mesh axis runs over, the one named last changes fastest.
Arguments:
- obs_values: bfloat16 [16384, 128], P(('lon', 'lat')), may hold values from -6 to 6
- obs_owner: int32 [16384, 1], P(('lon', 'lat')), may hold values from 0 to 7; in each aligned block of 512 rows (0 to 511, 512 to 1023, ...) at most 128 rows name the same one
- obs_cell: int32 [16384], P(('lon', 'lat')), may hold values from 0 to 2047
- obs_count: int32 [32], P(('lon', 'lat')), may hold values from 256 to 512, as said below
- obs_map: bfloat16 [128, 384], replicated, may hold values from -0.5 to 0.5
- column_mix: float32 [384, 384], replicated, may hold values from -0.3125 to 0.3125
- center: float32 [128, 512], P('lon', 'lat'), may hold values from 0.4 to 1
- neighbor: float32 [4, 128, 512], P(None, 'lon', 'lat'), may hold values from 0.08 to 0.3
Outputs:
- gradient: float32 [384, 128, 512], P(None, 'lon', 'lat')
Inputs may be any that keep to these rules, and one draw needn't show every extreme that they name: `obs_owner`: among the rows of one device at most 128 name the same longitude block, and some block is named by exactly 128 of them. `obs_count`: rows of a device past its count are not live; some device has all 512 rows live.
All inputs are finite; a program needn't handle non-finite values.
Results may differ from a plain program's by a relative error of at most 0.0029.
Values may be sent and summed in bfloat16 or wider, within the bound.
A program may use at most 64 MiB of HBM per device.

v0:
```python
import jax
import jax.numpy as jnp
from jax import lax
from jax.sharding import PartitionSpec as P

STEPS = 2


def with_halo(x, sides, width, wrap):
    for axis, dim in sides:
        size, length = (lax.axis_size(axis), x.shape[dim])
        up = [(i, (i + 1) % size) for i in range(size if wrap else size - 1)]
        down = [(j, i) for i, j in up]
        last = lax.slice_in_dim(x, length - width, length, axis=dim)
        first = lax.slice_in_dim(x, 0, width, axis=dim)
        before = lax.ppermute(last, axis, up)
        after = lax.ppermute(first, axis, down)
        x = jnp.concatenate([before, x, after], axis=dim)
    return x


def stencil(spread, middle, weights):
    return (
        middle * spread[:, 1:-1, 1:-1]
        + weights[0] * spread[:, :-2, 1:-1]
        + weights[1] * spread[:, 2:, 1:-1]
        + weights[2] * spread[:, 1:-1, :-2]
        + weights[3] * spread[:, 1:-1, 2:]
    )


def column_apply(mixing, adjoint):
    extent, lon_cells, lat_cells = adjoint.shape
    flat_cols = adjoint.reshape(extent, lon_cells * lat_cells)
    result = lax.dot_general(
        mixing,
        flat_cols,
        (((0,), (0,)), ((), ())),
        precision=lax.Precision.HIGHEST,
        preferred_element_type=jnp.float32,
    )
    return result.reshape(extent, lon_cells, lat_cells)


def on_device(obs_values, obs_owner, obs_cell, obs_count, obs_map, column_mix, center, neighbor):
    lon_count = lax.axis_size("lon")
    row_count = obs_values.shape[0]
    extent = column_mix.shape[0]
    capacity = 2 * row_count // lon_count
    slot_count = lon_count * capacity
    lon_cells, lat_cells = center.shape
    cell_count = lon_cells * lat_cells
    owners = obs_owner[:, 0]
    living = jnp.arange(row_count, dtype=jnp.int32) < obs_count[0]
    matches = (owners[:, None] == jnp.arange(lon_count, dtype=jnp.int32)[None, :]).astype(jnp.int32)
    earlier = jnp.sum(jnp.cumsum(matches, axis=0) * matches, axis=1) - 1
    target = owners * capacity + earlier
    places = jnp.where(living, obs_cell, -1)
    slot_places = (
        jnp.full((slot_count,), -1, jnp.int32).at[target].set(places).reshape(lon_count, capacity)
    )
    packed = (
        jnp.zeros((slot_count, extent), jnp.bfloat16)
        .at[target]
        .set(jnp.dot(obs_values, obs_map, preferred_element_type=jnp.float32).astype(jnp.bfloat16))
    )
    packed = packed.reshape(lon_count, capacity, extent)
    arrived, labels = (
        lax.all_to_all(packed, "lon", split_axis=0, concat_axis=0, tiled=True),
        lax.all_to_all(slot_places, "lon", split_axis=0, concat_axis=0, tiled=True),
    )
    block_rows = min(512, slot_count)
    batched = arrived.reshape(slot_count // block_rows, block_rows, extent)
    batched_places = labels.reshape(slot_count // block_rows, block_rows)
    targets = jnp.arange(cell_count, dtype=jnp.int32)

    def accumulate(running, element):
        values, places_in = element
        onehot = (places_in[:, None] == targets[None, :]).astype(jnp.bfloat16)
        update = lax.dot_general(
            values, onehot, (((0,), (0,)), ((), ())), preferred_element_type=jnp.float32
        )
        return (running + update, None)

    forcing, unused = lax.scan(
        accumulate, jnp.zeros((extent, cell_count), jnp.float32), (batched, batched_places)
    )
    adjoint = forcing.reshape(extent, lon_cells, lat_cells)
    for section in range(STEPS):
        mixed = column_apply(column_mix, adjoint)
        spread = with_halo(mixed, (("lon", 1),), 1, True)
        spread = with_halo(spread, (("lat", 2),), 1, False)
        adjoint = stencil(spread, center, neighbor)
    return adjoint


def solution(mesh):
    return jax.shard_map(
        on_device,
        mesh=mesh,
        in_specs=(
            P(("lon", "lat"), None),
            P(("lon", "lat"), None),
            P(("lon", "lat")),
            P(("lon", "lat")),
            P(),
            P(),
            P("lon", "lat"),
            P(None, "lon", "lat"),
        ),
        out_specs=P(None, "lon", "lat"),
        check_vma=False,
    )
```

profile of v0, /device:TPU:1, one launch (start us, length us, event | category | flops | bytes accessed | tf_op | source)
XLA Modules:
  0.0 137.6 jit_solution(2249607796687000426)
XLA Ops:
  0.0 0.7 fusion.26
  0.8 1.1 reduce-window.6
  1.9 0.2 slice_reduce_fusion
  2.1 0.8 fusion.25
  2.9 0.7 compare_select_fusion
  4.3 0.7 fusion.29
  4.9 3.0 %scatter_custom_fusion.1 = s32[1024]{0:T(1024)} fusion(s32[512]{0:T(512)S(1)} %bitcast.56, s32[512]{0:T(512)S(1)} %fusion.29, s32[]{:T(128)} %constant.17.clone.1), kind=kCustom, calls=%fused_computation.52 | custom fusion | bytes 4100 | tf_op jit(solution)/shard_map/scatter | solution.py:60
  8.0 6.4 %all-to-all-start.1 = ((s32[8,1,128]{2,1,0:T(1,128)}), s32[8,1,128]{2,1,0:T(1,128)S(1)}, u32[]{:S(2)}, u32[]{:S(2)}) async-start(s32[8,1,128]{2,1,0:T(1,128)} %bitcast.9), calls=%async_computation.1 | async-start | bytes 8192 | tf_op jit(solution)/shard_map/all_to_all | solution.py:70
  14.3 1.2 convolution_convert_fusion
  15.5 3.3 %scatter_custom_fusion = bf16[1024,384]{1,0:T(8,128)(2,1)} fusion(s32[512]{0:T(512)S(1)} %bitcast.57, bf16[512,384]{1,0:T(8,128)(2,1)S(1)} %convolution_convert_fusion, bf16[]{:T(256)} %constant.14.clone.1), kind=kCustom, calls=%fused_computation.38 | custom fusion | bytes 786434 | tf_op jit(solution)/shard_map/scatter | solution.py:65
  18.9 0.7 all-to-all-done.1
  19.6 4.7 %all-to-all-start = ((bf16[8,128,384]{2,1,0:T(8,128)(2,1)}), bf16[8,128,384]{2,1,0:T(8,128)(2,1)S(1)}, u32[]{:S(2)}, u32[]{:S(2)}) async-start(bf16[8,128,384]{2,1,0:T(8,128)(2,1)} %bitcast.6), calls=%async_computation | async-start | bytes 1572864 | tf_op jit(solution)/shard_map/all_to_all | solution.py:69
  24.3 0.5 broadcast.58
  24.8 0.6 reduce.5
  25.4 17.5 %all-to-all-done = bf16[8,128,384]{2,1,0:T(8,128)(2,1)S(1)} async-done(((bf16[8,128,384]{2,1,0:T(8,128)(2,1)}), bf16[8,128,384]{2,1,0:T(8,128)(2,1)S(1)}, u32[]{:S(2)}, u32[]{:S(2)}) %all-to-all-start) | async-done | bytes 786464 | tf_op jit(solution)/shard_map/all_to_all | solution.py:69
  42.9 7.7 %while.11 = (s32[]{:T(128)}, f32[384,2048]{1,0:T(8,128)}, bf16[2,512,384]{2,1,0:T(8,128)(2,1)S(1)}, s32[2,512]{1,0:T(2,128)S(1)}, s32[]{:T(128)}, /*index=5*/s32[]{:T(128)}) while((s32[]{:T(128)}, f32[384,2048]{1,0:T(8,128)}, bf16[2,512,384]{2,1,0:T(8,128)(2,1)S(1)}, s32[2,512]{1,0:T(2,128)S(1)}, s32[]{:T(128)}, ...), condition=%wide.region_6.7_spmd.clone, body=%wide.region_5.6_spmd.clone.sunk | while | flops 807927808 | bytes 6690911 | solution.py:85
  42.9 2.9 %select_add_fusion.2 = f32[384,2048]{1,0:T(8,128)} fusion(f32[384,2048]{1,0:T(8,128)} %get-tuple-element.102, s32[512]{0:T(512)S(1)} %bitcast.52, pred[]{:T(512)S(6)} %compare.3, bf16[2,512,384]{2,1,0:T(8,128)(2,1)S(1)} %get-tuple-element.109, s32[]{:T(128)S(6)} %copy.62), kind=kOutput, calls=%fused_computation.5.clone.1 | convolution fusion | flops 807927808 | bytes 6686725 | tf_op jit(solution)/shard_map/while/body/eval_jaxpr/dot_general | solution.py:80
  45.8 4.8 %select_add_fusion.2 = f32[384,2048]{1,0:T(8,128)} fusion(f32[384,2048]{1,0:T(8,128)} %get-tuple-element.102, s32[512]{0:T(512)S(1)} %bitcast.52, pred[]{:T(512)S(6)} %compare.3, bf16[2,512,384]{2,1,0:T(8,128)(2,1)S(1)} %get-tuple-element.109, s32[]{:T(128)S(6)} %copy.62), kind=kOutput, calls=%fused_computation.5.clone.1 | convolution fusion | flops 807927808 | bytes 6686725 | tf_op jit(solution)/shard_map/while/body/eval_jaxpr/dot_general | solution.py:80
  50.6 8.5 %fusion.34 = f32[2048,384]{1,0:T(8,128)S(1)} fusion(f32[384,2048]{1,0:T(8,128)} %get-tuple-element.32, f32[384,384]{1,0:T(8,128)S(1)} %copy-done), kind=kOutput, calls=%fused_computation.60 | convolution fusion | flops 3623878656 | bytes 6881280 | tf_op jit(solution)/shard_map/dot_general | solution.py:35
  59.1 1.7 %copy-done.1 = f32[2048,384]{1,0:T(8,128)} copy-done((f32[2048,384]{1,0:T(8,128)}, f32[2048,384]{1,0:T(8,128)S(1)}, u32[]{:S(2)}) %copy-start.1) | copy-done | bytes 3145752
  60.9 4.1 %collective-permute-start.1 = (f32[384,1,128]{2,0,1:T(8,128)S(1)}, f32[384,1,128]{2,0,1:T(8,128)S(1)}, u32[]{:S(2)}, u32[]{:S(2)}) collective-permute-start(f32[384,1,128]{2,0,1:T(8,128)S(1)} %copy.57), channel_id=1, source_target_pairs={{4,0},{8,4},{12,8},{16,12},{20,16},{24,20},{28,24},{0,28},{5,1},{9... | collective-permute-start | bytes 589832 | tf_op jit(solution)/shard_map/ppermute | solution.py:17
  65.2 0.2 collective-permute-start
  65.4 5.4 %copy.38 = f32[384,16,128]{0,1,2:T(8,128)} copy(f32[384,16,128]{0,2,1:T(8,128)} %bitcast.45) | data formatting | bytes 6291456 | tf_op jit(solution)/shard_map/reshape | solution.py:42
  70.8 0.2 copy.39
  71.0 2.8 %collective-permute-done = f32[384,1,128]{2,0,1:T(8,128)S(1)} collective-permute-done((f32[384,1,128]{2,0,1:T(8,128)S(1)}, f32[384,1,128]{2,0,1:T(8,128)S(1)}, u32[]{:S(2)}, u32[]{:S(2)}) %collective-permute-start) | collective-permute-done | bytes 196640 | tf_op jit(solution)/shard_map/ppermute | solution.py:16
  73.8 0.2 copy.37
  74.0 2.6 %pad_maximum_fusion = f32[384,18,128]{0,1,2:T(8,128)S(1)} fusion(f32[384,1,128]{0,1,2:T(1,128)S(1)} %copy.39, f32[384,16,128]{0,1,2:T(8,128)} %copy.38, f32[384,1,128]{0,1,2:T(1,128)S(1)} %copy.37), kind=kLoop, calls=%fused_computation.11 | loop fusion | flops 1769472 | bytes 7077888 | tf_op jit(solution)/shard_map/concatenate | solution.py:18
  76.6 3.6 %collective-permute-start.3 = (f32[384,18,1]{0,1,2:T(8,128)S(1)}, f32[384,18,1]{0,1,2:T(8,128)S(1)}, u32[]{:S(2)}, u32[]{:S(2)}) collective-permute-start(f32[384,18,1]{0,1,2:T(8,128)S(1)} %get-tuple-element.61), channel_id=1, source_target_pairs={{1,0},{2,1},{3,2},{5,4},{6,5},{7,6},{9,8},{10,9},{11,10},{13,12},{... | collective-permute-start | bytes 82952 | tf_op jit(solution)/shard_map/ppermute | solution.py:17
  80.1 3.0 %collective-permute-start.2 = (f32[384,18,1]{0,1,2:T(8,128)S(1)}, f32[384,18,1]{0,1,2:T(8,128)S(1)}, u32[]{:S(2)}, u32[]{:S(2)}) collective-permute-start(f32[384,18,1]{0,1,2:T(8,128)S(1)} %get-tuple-element.60), channel_id=1, source_target_pairs={{0,1},{1,2},{2,3},{4,5},{5,6},{6,7},{8,9},{9,10},{10,11},{12,13},{... | collective-permute-start | bytes 82952 | tf_op jit(solution)/shard_map/ppermute | solution.py:16
  83.2 2.4 %copy.41 = f32[384,18,128]{0,2,1:T(8,128)} copy(f32[384,18,128]{0,1,2:T(8,128)S(1)} %pad_maximum_fusion) | data formatting | bytes 7077888 | tf_op jit(solution)/shard_map/concatenate | solution.py:18
  85.6 0.1 copy.36
  85.7 0.1 copy.34
  85.9 7.9 %fusion.16 = f32[384,16,128]{0,2,1:T(8,128)S(1)} fusion(f32[384,18,1]{0,2,1:T(1,128)S(1)} %copy.43, f32[384,18,128]{0,2,1:T(8,128)} %copy.41, f32[384,18,1]{0,2,1:T(1,128)S(1)} %copy.40, f32[384,1,128]{0,2,1:T(8,128)S(1)} %copy.36, f32[384,16,128]{0,2,1:T(8,128)} %bitcast.46, f32[384,1,128]{0,2,1:T(8,128)S(1)} %copy.34, f32[16,128]{1,0:T(8,128)S(1)} %get-tuple-element.68, ...), kind=kLoop, calls=%fused_computation.27 | loop fusion | flops 10223616 | bytes 10319872 | tf_op jit(solution)/shard_map/add | solution.py:24
  93.8 6.7 %fusion.35 = f32[2048,384]{1,0:T(8,128)S(1)} fusion(f32[384,2048]{0,1:T(8,128)S(1)} %bitcast.50, f32[384,384]{1,0:T(8,128)S(1)} %copy-done), kind=kOutput, calls=%fused_computation.61 | convolution fusion | flops 3623878656 | bytes 6881280 | tf_op jit(solution)/shard_map/dot_general | solution.py:35
  100.5 1.7 %copy-done.2 = f32[2048,384]{1,0:T(8,128)} copy-done((f32[2048,384]{1,0:T(8,128)}, f32[2048,384]{1,0:T(8,128)S(1)}, u32[]{:S(2)}) %copy-start.2) | copy-done | bytes 3145752
  102.4 1.6 %collective-permute-start.5 = (f32[384,1,128]{2,0,1:T(8,128)S(1)}, f32[384,1,128]{2,0,1:T(8,128)S(1)}, u32[]{:S(2)}, u32[]{:S(2)}) collective-permute-start(f32[384,1,128]{2,0,1:T(8,128)S(1)} %copy.59), channel_id=1, source_target_pairs={{4,0},{8,4},{12,8},{16,12},{20,16},{24,20},{28,24},{0,28},{5,1},{9... | collective-permute-start | bytes 589832 | tf_op jit(solution)/shard_map/ppermute | solution.py:17
  104.1 0.3 collective-permute-start.4
  104.4 5.4 %copy.49 = f32[384,16,128]{0,1,2:T(8,128)} copy(f32[384,16,128]{0,2,1:T(8,128)} %bitcast.48) | data formatting | bytes 6291456 | tf_op jit(solution)/shard_map/reshape | solution.py:42
  109.7 0.2 copy.50
  109.9 3.9 %collective-permute-done.4 = f32[384,1,128]{2,0,1:T(8,128)S(1)} collective-permute-done((f32[384,1,128]{2,0,1:T(8,128)S(1)}, f32[384,1,128]{2,0,1:T(8,128)S(1)}, u32[]{:S(2)}, u32[]{:S(2)}) %collective-permute-start.4) | collective-permute-done | bytes 196640 | tf_op jit(solution)/shard_map/ppermute | solution.py:16
  113.8 0.2 copy.48
  114.0 2.6 %pad_maximum_fusion.1 = f32[384,18,128]{0,1,2:T(8,128)S(1)} fusion(f32[384,1,128]{0,1,2:T(1,128)S(1)} %copy.50, f32[384,16,128]{0,1,2:T(8,128)} %copy.49, f32[384,1,128]{0,1,2:T(1,128)S(1)} %copy.48), kind=kLoop, calls=%fused_computation.12 | loop fusion | flops 1769472 | bytes 7077888 | tf_op jit(solution)/shard_map/concatenate | solution.py:18
  116.6 2.5 %collective-permute-start.7 = (f32[384,18,1]{0,1,2:T(8,128)S(1)}, f32[384,18,1]{0,1,2:T(8,128)S(1)}, u32[]{:S(2)}, u32[]{:S(2)}) collective-permute-start(f32[384,18,1]{0,1,2:T(8,128)S(1)} %get-tuple-element.59), channel_id=1, source_target_pairs={{1,0},{2,1},{3,2},{5,4},{6,5},{7,6},{9,8},{10,9},{11,10},{13,12},{... | collective-permute-start | bytes 82952 | tf_op jit(solution)/shard_map/ppermute | solution.py:17
  119.1 3.1 %collective-permute-start.6 = (f32[384,18,1]{0,1,2:T(8,128)S(1)}, f32[384,18,1]{0,1,2:T(8,128)S(1)}, u32[]{:S(2)}, u32[]{:S(2)}) collective-permute-start(f32[384,18,1]{0,1,2:T(8,128)S(1)} %get-tuple-element.58), channel_id=1, source_target_pairs={{0,1},{1,2},{2,3},{4,5},{5,6},{6,7},{8,9},{9,10},{10,11},{12,13},{... | collective-permute-start | bytes 82952 | tf_op jit(solution)/shard_map/ppermute | solution.py:16
  122.2 2.4 %copy.52 = f32[384,18,128]{0,2,1:T(8,128)} copy(f32[384,18,128]{0,1,2:T(8,128)S(1)} %pad_maximum_fusion.1) | data formatting | bytes 7077888 | tf_op jit(solution)/shard_map/concatenate | solution.py:18
  124.7 0.1 copy.45
  124.9 9.1 %fusion.8 = f32[384,16,128]{0,2,1:T(8,128)} fusion(f32[384,18,1]{0,2,1:T(1,128)S(1)} %copy.54, f32[384,18,128]{0,2,1:T(8,128)} %copy.52, f32[384,18,1]{0,2,1:T(1,128)S(1)} %copy.51, f32[384,1,128]{0,2,1:T(8,128)S(1)} %copy.47, f32[384,16,128]{0,2,1:T(8,128)} %bitcast.49, f32[384,1,128]{0,2,1:T(8,128)S(1)} %copy.45, f32[16,128]{1,0:T(8,128)S(1)} %get-tuple-element.68, ...), kind=kLoop, calls=%fused_computation.15 | loop fusion | flops 10223616 | bytes 10319872 | tf_op jit(solution)/shard_map/add | solution.py:24
  134.0 3.5 %copy.55 = f32[384,16,128]{2,1,0:T(8,128)} copy(f32[384,16,128]{0,2,1:T(8,128)} %fusion.8) | data formatting | bytes 6291456 | tf_op jit(solution)/shard_map/add | solution.py:24
  (35 shorter events, 0.9 us)
Async XLA Ops:
  0.0 50.6 %copy-start = (f32[384,384]{1,0:T(8,128)S(1)}, f32[384,384]{1,0:T(8,128)}, u32[]{:S(2)}) copy-start(f32[384,384]{1,0:T(8,128)} %param.15) | copy-start | bytes 1769476
  8.0 11.6 %all-to-all-start.1 = ((s32[8,1,128]{2,1,0:T(1,128)}), s32[8,1,128]{2,1,0:T(1,128)S(1)}, u32[]{:S(2)}, u32[]{:S(2)}) async-start(s32[8,1,128]{2,1,0:T(1,128)} %bitcast.9), calls=%async_computation.1 | async-start | bytes 8192 | tf_op jit(solution)/shard_map/all_to_all | solution.py:70
  19.6 23.3 %all-to-all-start = ((bf16[8,128,384]{2,1,0:T(8,128)(2,1)}), bf16[8,128,384]{2,1,0:T(8,128)(2,1)S(1)}, u32[]{:S(2)}, u32[]{:S(2)}) async-start(bf16[8,128,384]{2,1,0:T(8,128)(2,1)} %bitcast.6), calls=%async_computation | async-start | bytes 1572864 | tf_op jit(solution)/shard_map/all_to_all | solution.py:69
  59.1 1.7 %copy-start.1 = (f32[2048,384]{1,0:T(8,128)}, f32[2048,384]{1,0:T(8,128)S(1)}, u32[]{:S(2)}) copy-start(f32[2048,384]{1,0:T(8,128)S(1)} %fusion.34) | copy-start | bytes 9437188
  60.9 9.9 %collective-permute-start.1 = (f32[384,1,128]{2,0,1:T(8,128)S(1)}, f32[384,1,128]{2,0,1:T(8,128)S(1)}, u32[]{:S(2)}, u32[]{:S(2)}) collective-permute-start(f32[384,1,128]{2,0,1:T(8,128)S(1)} %copy.57), channel_id=1, source_target_pairs={{4,0},{8,4},{12,8},{16,12},{20,16},{24,20},{28,24},{0,28},{5,1},{9... | collective-permute-start | bytes 589832 | tf_op jit(solution)/shard_map/ppermute | solution.py:17
  65.2 8.6 %collective-permute-start = (f32[384,1,128]{2,0,1:T(8,128)S(1)}, f32[384,1,128]{2,0,1:T(8,128)S(1)}, u32[]{:S(2)}, u32[]{:S(2)}) collective-permute-start(f32[384,1,128]{2,0,1:T(8,128)S(1)} %copy.56), channel_id=1, source_target_pairs={{0,4},{4,8},{8,12},{12,16},{16,20},{20,24},{24,28},{28,0},{1,5},{5... | collective-permute-start | bytes 589832 | tf_op jit(solution)/shard_map/ppermute | solution.py:16
  73.9 9.2 %copy-start.4 = (f32[4,16,128]{2,1,0:T(8,128)S(1)}, f32[4,16,128]{2,1,0:T(8,128)}, u32[]{:S(2)}) copy-start(f32[4,16,128]{2,1,0:T(8,128)} %param.17) | copy-start | bytes 98308
  76.6 9.3 %collective-permute-start.3 = (f32[384,18,1]{0,1,2:T(8,128)S(1)}, f32[384,18,1]{0,1,2:T(8,128)S(1)}, u32[]{:S(2)}, u32[]{:S(2)}) collective-permute-start(f32[384,18,1]{0,1,2:T(8,128)S(1)} %get-tuple-element.61), channel_id=1, source_target_pairs={{1,0},{2,1},{3,2},{5,4},{6,5},{7,6},{9,8},{10,9},{11,10},{13,12},{... | collective-permute-start | bytes 82952 | tf_op jit(solution)/shard_map/ppermute | solution.py:17
  80.1 5.8 %collective-permute-start.2 = (f32[384,18,1]{0,1,2:T(8,128)S(1)}, f32[384,18,1]{0,1,2:T(8,128)S(1)}, u32[]{:S(2)}, u32[]{:S(2)}) collective-permute-start(f32[384,18,1]{0,1,2:T(8,128)S(1)} %get-tuple-element.60), channel_id=1, source_target_pairs={{0,1},{1,2},{2,3},{4,5},{5,6},{6,7},{8,9},{9,10},{10,11},{12,13},{... | collective-permute-start | bytes 82952 | tf_op jit(solution)/shard_map/ppermute | solution.py:16
  83.2 2.8 %copy-start.3 = (f32[16,128]{1,0:T(8,128)S(1)}, f32[16,128]{1,0:T(8,128)}, u32[]{:S(2)}) copy-start(f32[16,128]{1,0:T(8,128)} %param.16) | copy-start | bytes 24580
  100.5 1.7 %copy-start.2 = (f32[2048,384]{1,0:T(8,128)}, f32[2048,384]{1,0:T(8,128)S(1)}, u32[]{:S(2)}) copy-start(f32[2048,384]{1,0:T(8,128)S(1)} %fusion.35) | copy-start | bytes 9437188
  102.4 7.4 %collective-permute-start.5 = (f32[384,1,128]{2,0,1:T(8,128)S(1)}, f32[384,1,128]{2,0,1:T(8,128)S(1)}, u32[]{:S(2)}, u32[]{:S(2)}) collective-permute-start(f32[384,1,128]{2,0,1:T(8,128)S(1)} %copy.59), channel_id=1, source_target_pairs={{4,0},{8,4},{12,8},{16,12},{20,16},{24,20},{28,24},{0,28},{5,1},{9... | collective-permute-start | bytes 589832 | tf_op jit(solution)/shard_map/ppermute | solution.py:17
  104.1 9.7 %collective-permute-start.4 = (f32[384,1,128]{2,0,1:T(8,128)S(1)}, f32[384,1,128]{2,0,1:T(8,128)S(1)}, u32[]{:S(2)}, u32[]{:S(2)}) collective-permute-start(f32[384,1,128]{2,0,1:T(8,128)S(1)} %copy.58), channel_id=1, source_target_pairs={{0,4},{4,8},{8,12},{12,16},{16,20},{20,24},{24,28},{28,0},{1,5},{5... | collective-permute-start | bytes 589832 | tf_op jit(solution)/shard_map/ppermute | solution.py:16
  116.6 8.2 %collective-permute-start.7 = (f32[384,18,1]{0,1,2:T(8,128)S(1)}, f32[384,18,1]{0,1,2:T(8,128)S(1)}, u32[]{:S(2)}, u32[]{:S(2)}) collective-permute-start(f32[384,18,1]{0,1,2:T(8,128)S(1)} %get-tuple-element.59), channel_id=1, source_target_pairs={{1,0},{2,1},{3,2},{5,4},{6,5},{7,6},{9,8},{10,9},{11,10},{13,12},{... | collective-permute-start | bytes 82952 | tf_op jit(solution)/shard_map/ppermute | solution.py:17
  119.1 5.8 %collective-permute-start.6 = (f32[384,18,1]{0,1,2:T(8,128)S(1)}, f32[384,18,1]{0,1,2:T(8,128)S(1)}, u32[]{:S(2)}, u32[]{:S(2)}) collective-permute-start(f32[384,18,1]{0,1,2:T(8,128)S(1)} %get-tuple-element.58), channel_id=1, source_target_pairs={{0,1},{1,2},{2,3},{4,5},{5,6},{6,7},{8,9},{9,10},{10,11},{12,13},{... | collective-permute-start | bytes 82952 | tf_op jit(solution)/shard_map/ppermute | solution.py:16
where the time goes:
time: 138 us
  local copies, waits for them, and re-layouts  31.3 us (23%)
  starting transfers between devices  29.5 us (21%)
  other arithmetic  26.8 us (19%)
  waiting for transfers between devices  25 us (18%)
  matrix products  24.1 us (17%)
    all_to_all x1, waiting for transfers between devices, on_device(): lax.all_to_all(packed, 'lon', split_axis=0, concat_axis=0, tiled=True)  17.5 us
    add x2, other arithmetic, stencil(): middle * spread[:, 1:-1, 1:-1] + weights[0] * spread[:, :-2, 1:-1]  17 us
    dot_general x2, matrix products, column_apply(): lax.dot_general(mixing, flat_cols, (((0,), (0,)), ((), ())), precision=la...  15.2 us
    ppermute x4, starting transfers between devices, with_halo(): after = lax.ppermute(first, axis, down)  11.7 us
    reshape x2, local copies, waits for them, and re-layouts, column_apply(): return result.reshape(extent, lon_cells, lat_cells)  10.7 us
    dot_general x2, matrix products, accumulate(): lax.dot_general(values, onehot, (((0,), (0,)), ((), ())), preferred_eleme...  7.72 us
    ppermute x4, waiting for transfers between devices, with_halo(): before = lax.ppermute(last, axis, up)  6.75 us
    ppermute x4, starting transfers between devices, with_halo(): before = lax.ppermute(last, axis, up)  6.63 us
  transfers between devices with their start and end apart: 10, of which 4 were waited for; matrix products, arithmetic and copies ran while one was open for 16% of the time, Pallas kernels for 0%

commit v1 on v0

--- a/solution.py
+++ b/solution.py
@@ -4,6 +4,28 @@
 from jax.sharding import PartitionSpec as P
 
 STEPS = 2
+
+
+def assign_unit(q_in, ax_name, at_axis, ndim_at):
+    reached = jax.lax.psum(1, ax_name)
+    y2 = jax.lax.axis_index(ax_name)
+    k_now, ready = (reached, y2)
+    all_rows = q_in.shape[at_axis] // k_now
+    carry_in = list(q_in.shape)
+    carry_in[at_axis] = all_rows
+    shaped = carry_in[ndim_at]
+    carry_in[ndim_at] = shaped * k_now
+    block_last = jnp.zeros(carry_in, q_in.dtype)
+    for s in [*range(k_now)]:
+        block_now = lax.dynamic_slice_in_dim(q_in, (ready ^ s) * all_rows, all_rows, axis=at_axis)
+        if s:
+            block_now = jax.lax.ppermute(
+                block_now, axis_name=ax_name, perm=[(b, b ^ s) for b in range(k_now)]
+            )
+        block_last = lax.dynamic_update_slice_in_dim(
+            block_last, block_now, (ready ^ s) * shaped, axis=ndim_at
+        )
+    return block_last
 
 
 def with_halo(x, sides, width, wrap):
@@ -67,7 +89,7 @@
     packed = packed.reshape(lon_count, capacity, extent)
     arrived, labels = (
         lax.all_to_all(packed, "lon", split_axis=0, concat_axis=0, tiled=True),
-        lax.all_to_all(slot_places, "lon", split_axis=0, concat_axis=0, tiled=True),
+        assign_unit(slot_places, "lon", 0, 0),
     )
     block_rows = min(512, slot_count)
     batched = arrived.reshape(slot_count // block_rows, block_rows, extent)

time: 138 us -> 129 us (0.935)
  waiting for transfers between devices: 25 us -> 10 us
  starting transfers between devices: 29.5 us -> 37.5 us
  other arithmetic: 26.8 us -> 25.4 us
    all_to_all x1, waiting for transfers between devices: 17.5 us -> 0.01 us  [on_device(): lax.all_to_all(packed, 'lon', split_axis=0, concat_axis=0, tiled=True)]
    ppermute x0 -> x7, starting transfers between devices: none -> 13 us  [assign_unit(): jax.lax.ppermute(block_now, axis_name=ax_name, perm=[(b, b ^ s) for b in...]
    all_to_all x1 -> x0, starting transfers between devices: 6.38 us -> none  [on_device(): lax.all_to_all(slot_places, 'lon', split_axis=0, concat_axis=0, tiled=True)]
    ppermute x0 -> x7, waiting for transfers between devices: none -> 3.89 us  [assign_unit(): jax.lax.ppermute(block_now, axis_name=ax_name, perm=[(b, b ^ s) for b in...]
    all_to_all x1, starting transfers between devices: 4.72 us -> 6.38 us  [on_device(): lax.all_to_all(packed, 'lon', split_axis=0, concat_axis=0, tiled=True)]
    unnamed x14 -> x16, local copies, waits for them, and re-layouts: 3.82 us -> 3.82 us
  transfers between devices with their start and end apart: 10 -> 16, of which waited for: 4 -> 4; matrix products, arithmetic and copies ran while one was open for 16% -> 15% of each run, Pallas kernels for 0% -> 0%
where the time goes in v1:
time: 129 us
  starting transfers between devices  37.5 us (29%)
  local copies, waits for them, and re-layouts  30.6 us (24%)
  other arithmetic  25.4 us (20%)
  matrix products  24.1 us (19%)
  waiting for transfers between devices  10 us (8%)
    add x2, other arithmetic, stencil(): middle * spread[:, 1:-1, 1:-1] + weights[0] * spread[:, :-2, 1:-1]  16.8 us
    dot_general x2, matrix products, column_apply(): lax.dot_general(mixing, flat_cols, (((0,), (0,)), ((), ())), precision=la...  15.2 us
    ppermute x7, starting transfers between devices, assign_unit(): jax.lax.ppermute(block_now, axis_name=ax_name, perm=[(b, b ^ s) for b in...  13 us
    ppermute x4, starting transfers between devices, with_halo(): after = lax.ppermute(first, axis, down)  11.6 us
    reshape x2, local copies, waits for them, and re-layouts, column_apply(): return result.reshape(extent, lon_cells, lat_cells)  10.7 us
    dot_general x2, matrix products, accumulate(): lax.dot_general(values, onehot, (((0,), (0,)), ((), ())), preferred_eleme...  7.72 us
    ppermute x4, starting transfers between devices, with_halo(): before = lax.ppermute(last, axis, up)  6.47 us
    all_to_all x1, starting transfers between devices, on_device(): lax.all_to_all(packed, 'lon', split_axis=0, concat_axis=0, tiled=True)  6.38 us
  transfers between devices with their start and end apart: 16, of which 4 were waited for; matrix products, arithmetic and copies ran while one was open for 15% of the time, Pallas kernels for 0%

profile of v1, /device:TPU:1, one launch (start us, length us, event | category | flops | bytes accessed | tf_op | source)
XLA Modules:
  0.0 128.7 jit_solution(10752246021187578912)
XLA Ops:
  0.0 0.8 fusion.26
  0.8 1.1 reduce-window.6
  1.9 0.2 slice_reduce_fusion
  2.2 0.8 fusion.25
  2.9 0.7 compare_select_fusion
  3.6 1.2 convolution_convert_fusion
  4.8 3.3 %scatter_custom_fusion = bf16[1024,384]{1,0:T(8,128)(2,1)} fusion(s32[512]{0:T(512)S(1)} %bitcast.57, bf16[512,384]{1,0:T(8,128)(2,1)S(1)} %convolution_convert_fusion, bf16[]{:T(256)} %constant.9.clone.1), kind=kCustom, calls=%fused_computation.38 | custom fusion | bytes 786434 | tf_op jit(solution)/shard_map/scatter | solution.py:87
  8.2 6.4 %all-to-all-start = ((bf16[8,128,384]{2,1,0:T(8,128)(2,1)}), bf16[8,128,384]{2,1,0:T(8,128)(2,1)S(1)}, u32[]{:S(2)}, u32[]{:S(2)}) async-start(bf16[8,128,384]{2,1,0:T(8,128)(2,1)} %bitcast.6), calls=%async_computation | async-start | bytes 1572864 | tf_op jit(solution)/shard_map/all_to_all | solution.py:91
  15.2 2.4 %scatter_custom_fusion.1 = s32[1024]{0:T(1024)S(1)} fusion(s32[512]{0:T(512)S(1)} %bitcast.58, s32[512]{0:T(512)S(1)} %fusion.29, s32[]{:T(128)} %constant.10.clone.1), kind=kCustom, calls=%fused_computation.52 | custom fusion | bytes 4100 | tf_op jit(solution)/shard_map/scatter | solution.py:82
  17.7 1.5 %collective-permute-start = (s32[1,128]{1,0:T(1,128)S(1)}, s32[1,128]{1,0:T(1,128)S(1)}, u32[]{:S(2)}, u32[]{:S(2)}) collective-permute-start(s32[1,128]{1,0:T(1,128)S(1)} %get-tuple-element.76), channel_id=1, source_target_pairs={{0,4},{4,0},{8,12},{12,8},{16,20},{20,16},{24,28},{28,24},{1,5},{5... | collective-permute-start | bytes 1544 | tf_op jit(solution)/shard_map/ppermute | solution.py:22
  19.3 1.2 collective-permute-start.1
  20.5 2.3 %collective-permute-start.3 = (s32[1,128]{1,0:T(1,128)S(1)}, s32[1,128]{1,0:T(1,128)S(1)}, u32[]{:S(2)}, u32[]{:S(2)}) collective-permute-start(s32[1,128]{1,0:T(1,128)S(1)} %get-tuple-element.73), channel_id=1, source_target_pairs={{0,16},{4,20},{8,24},{12,28},{16,0},{20,4},{24,8},{28,12},{1,17},{... | collective-permute-start | bytes 1544 | tf_op jit(solution)/shard_map/ppermute | solution.py:22
  22.8 1.2 collective-permute-start.4
  24.0 3.0 %collective-permute-start.5 = (s32[1,128]{1,0:T(1,128)S(1)}, s32[1,128]{1,0:T(1,128)S(1)}, u32[]{:S(2)}, u32[]{:S(2)}) collective-permute-start(s32[1,128]{1,0:T(1,128)S(1)} %get-tuple-element.71), channel_id=1, source_target_pairs={{0,24},{4,28},{8,16},{12,20},{16,8},{20,12},{24,0},{28,4},{1,25},{... | collective-permute-start | bytes 1544 | tf_op jit(solution)/shard_map/ppermute | solution.py:22
  27.1 3.7 %collective-permute-start.6 = (s32[1,128]{1,0:T(1,128)S(1)}, s32[1,128]{1,0:T(1,128)S(1)}, u32[]{:S(2)}, u32[]{:S(2)}) collective-permute-start(s32[1,128]{1,0:T(1,128)S(1)} %get-tuple-element.70), channel_id=1, source_target_pairs={{0,28},{4,24},{8,20},{12,16},{16,12},{20,8},{24,4},{28,0},{1,29},{... | collective-permute-start | bytes 1544 | tf_op jit(solution)/shard_map/ppermute | solution.py:22
  30.9 2.8 %collective-permute-done.3 = s32[1,128]{1,0:T(1,128)S(1)} collective-permute-done((s32[1,128]{1,0:T(1,128)S(1)}, s32[1,128]{1,0:T(1,128)S(1)}, u32[]{:S(2)}, u32[]{:S(2)}) %collective-permute-start.3) | collective-permute-done | bytes 544 | tf_op jit(solution)/shard_map/ppermute | solution.py:22
  33.7 1.1 collective-permute-done.4
  34.9 0.2 dynamic_update_slice.31
  35.1 7.8 %while.11 = (s32[]{:T(128)}, f32[384,2048]{1,0:T(8,128)}, bf16[2,512,384]{2,1,0:T(8,128)(2,1)S(1)}, s32[2,512]{1,0:T(2,128)S(1)}, s32[]{:T(128)}, /*index=5*/s32[]{:T(128)}) while((s32[]{:T(128)}, f32[384,2048]{1,0:T(8,128)}, bf16[2,512,384]{2,1,0:T(8,128)(2,1)S(1)}, s32[2,512]{1,0:T(2,128)S(1)}, s32[]{:T(128)}, ...), condition=%wide.region_6.7_spmd.clone, body=%wide.region_5.6_spmd.clone.sunk | while | flops 807927808 | bytes 6690911 | solution.py:107
  35.1 2.9 %select_add_fusion.2 = f32[384,2048]{1,0:T(8,128)} fusion(f32[384,2048]{1,0:T(8,128)} %get-tuple-element.110, s32[512]{0:T(512)S(1)} %bitcast.52, pred[]{:T(512)S(6)} %compare.3, bf16[2,512,384]{2,1,0:T(8,128)(2,1)S(1)} %get-tuple-element.117, s32[]{:T(128)S(6)} %copy.70), kind=kOutput, calls=%fused_computation.5.clone.1 | convolution fusion | flops 807927808 | bytes 6686725 | tf_op jit(solution)/shard_map/while/body/eval_jaxpr/dot_general | solution.py:102
  38.1 4.8 %select_add_fusion.2 = f32[384,2048]{1,0:T(8,128)} fusion(f32[384,2048]{1,0:T(8,128)} %get-tuple-element.110, s32[512]{0:T(512)S(1)} %bitcast.52, pred[]{:T(512)S(6)} %compare.3, bf16[2,512,384]{2,1,0:T(8,128)(2,1)S(1)} %get-tuple-element.117, s32[]{:T(128)S(6)} %copy.70), kind=kOutput, calls=%fused_computation.5.clone.1 | convolution fusion | flops 807927808 | bytes 6686725 | tf_op jit(solution)/shard_map/while/body/eval_jaxpr/dot_general | solution.py:102
  42.9 8.5 %fusion.34 = f32[2048,384]{1,0:T(8,128)S(1)} fusion(f32[384,2048]{1,0:T(8,128)} %get-tuple-element.32, f32[384,384]{1,0:T(8,128)S(1)} %copy-done), kind=kOutput, calls=%fused_computation.68 | convolution fusion | flops 3623878656 | bytes 6881280 | tf_op jit(solution)/shard_map/dot_general | solution.py:57
  51.3 1.7 %copy-done.1 = f32[2048,384]{1,0:T(8,128)} copy-done((f32[2048,384]{1,0:T(8,128)}, f32[2048,384]{1,0:T(8,128)S(1)}, u32[]{:S(2)}) %copy-start.1) | copy-done | bytes 3145752
  53.2 2.5 %collective-permute-start.8 = (f32[384,1,128]{2,0,1:T(8,128)S(1)}, f32[384,1,128]{2,0,1:T(8,128)S(1)}, u32[]{:S(2)}, u32[]{:S(2)}) collective-permute-start(f32[384,1,128]{2,0,1:T(8,128)S(1)} %copy.57), channel_id=1, source_target_pairs={{4,0},{8,4},{12,8},{16,12},{20,16},{24,20},{28,24},{0,28},{5,1},{9... | collective-permute-start | bytes 589832 | tf_op jit(solution)/shard_map/ppermute | solution.py:39
  55.9 5.3 %copy.38 = f32[384,16,128]{0,1,2:T(8,128)} copy(f32[384,16,128]{0,2,1:T(8,128)} %bitcast.45) | data formatting | bytes 6291456 | tf_op jit(solution)/shard_map/reshape | solution.py:64
  61.2 0.2 copy.39
  61.4 2.2 %collective-permute-done.7 = f32[384,1,128]{2,0,1:T(8,128)S(1)} collective-permute-done((f32[384,1,128]{2,0,1:T(8,128)S(1)}, f32[384,1,128]{2,0,1:T(8,128)S(1)}, u32[]{:S(2)}, u32[]{:S(2)}) %collective-permute-start.7) | collective-permute-done | bytes 196640 | tf_op jit(solution)/shard_map/ppermute | solution.py:38
  63.6 0.2 copy.37
  63.8 2.6 %pad_maximum_fusion = f32[384,18,128]{0,1,2:T(8,128)S(1)} fusion(f32[384,1,128]{0,1,2:T(1,128)S(1)} %copy.39, f32[384,16,128]{0,1,2:T(8,128)} %copy.38, f32[384,1,128]{0,1,2:T(1,128)S(1)} %copy.37), kind=kLoop, calls=%fused_computation.11 | loop fusion | flops 1769472 | bytes 7077888 | tf_op jit(solution)/shard_map/concatenate | solution.py:40
  66.4 4.4 %collective-permute-start.10 = (f32[384,18,1]{0,1,2:T(8,128)S(1)}, f32[384,18,1]{0,1,2:T(8,128)S(1)}, u32[]{:S(2)}, u32[]{:S(2)}) collective-permute-start(f32[384,18,1]{0,1,2:T(8,128)S(1)} %get-tuple-element.61), channel_id=1, source_target_pairs={{1,0},{2,1},{3,2},{5,4},{6,5},{7,6},{9,8},{10,9},{11,10},{13,12},{... | collective-permute-start | bytes 82952 | tf_op jit(solution)/shard_map/ppermute | solution.py:39
  70.7 3.2 %collective-permute-start.9 = (f32[384,18,1]{0,1,2:T(8,128)S(1)}, f32[384,18,1]{0,1,2:T(8,128)S(1)}, u32[]{:S(2)}, u32[]{:S(2)}) collective-permute-start(f32[384,18,1]{0,1,2:T(8,128)S(1)} %get-tuple-element.60), channel_id=1, source_target_pairs={{0,1},{1,2},{2,3},{4,5},{5,6},{6,7},{8,9},{9,10},{10,11},{12,13},{... | collective-permute-start | bytes 82952 | tf_op jit(solution)/shard_map/ppermute | solution.py:38
  74.0 2.4 %copy.41 = f32[384,18,128]{0,2,1:T(8,128)} copy(f32[384,18,128]{0,1,2:T(8,128)S(1)} %pad_maximum_fusion) | data formatting | bytes 7077888 | tf_op jit(solution)/shard_map/concatenate | solution.py:40
  76.5 0.1 copy.34
  76.8 7.8 %fusion.16 = f32[384,16,128]{0,2,1:T(8,128)S(1)} fusion(f32[384,18,1]{0,2,1:T(1,128)S(1)} %copy.43, f32[384,18,128]{0,2,1:T(8,128)} %copy.41, f32[384,18,1]{0,2,1:T(1,128)S(1)} %copy.40, f32[384,1,128]{0,2,1:T(8,128)S(1)} %copy.36, f32[384,16,128]{0,2,1:T(8,128)} %bitcast.46, f32[384,1,128]{0,2,1:T(8,128)S(1)} %copy.34, f32[16,128]{1,0:T(8,128)S(1)} %get-tuple-element.68, ...), kind=kLoop, calls=%fused_computation.27 | loop fusion | flops 10223616 | bytes 10319872 | tf_op jit(solution)/shard_map/add | solution.py:46
  84.6 6.7 %fusion.35 = f32[2048,384]{1,0:T(8,128)S(1)} fusion(f32[384,2048]{0,1:T(8,128)S(1)} %bitcast.50, f32[384,384]{1,0:T(8,128)S(1)} %copy-done), kind=kOutput, calls=%fused_computation.69 | convolution fusion | flops 3623878656 | bytes 6881280 | tf_op jit(solution)/shard_map/dot_general | solution.py:57
  91.3 1.7 %copy-done.2 = f32[2048,384]{1,0:T(8,128)} copy-done((f32[2048,384]{1,0:T(8,128)}, f32[2048,384]{1,0:T(8,128)S(1)}, u32[]{:S(2)}) %copy-start.2) | copy-done | bytes 3145752
  93.1 2.3 %collective-permute-start.12 = (f32[384,1,128]{2,0,1:T(8,128)S(1)}, f32[384,1,128]{2,0,1:T(8,128)S(1)}, u32[]{:S(2)}, u32[]{:S(2)}) collective-permute-start(f32[384,1,128]{2,0,1:T(8,128)S(1)} %copy.59), channel_id=1, source_target_pairs={{4,0},{8,4},{12,8},{16,12},{20,16},{24,20},{28,24},{0,28},{5,1},{9... | collective-permute-start | bytes 589832 | tf_op jit(solution)/shard_map/ppermute | solution.py:39
  95.6 5.3 %copy.49 = f32[384,16,128]{0,1,2:T(8,128)} copy(f32[384,16,128]{0,2,1:T(8,128)} %bitcast.48) | data formatting | bytes 6291456 | tf_op jit(solution)/shard_map/reshape | solution.py:64
  101.0 0.2 copy.50
  101.1 3.9 %collective-permute-done.11 = f32[384,1,128]{2,0,1:T(8,128)S(1)} collective-permute-done((f32[384,1,128]{2,0,1:T(8,128)S(1)}, f32[384,1,128]{2,0,1:T(8,128)S(1)}, u32[]{:S(2)}, u32[]{:S(2)}) %collective-permute-start.11) | collective-permute-done | bytes 196640 | tf_op jit(solution)/shard_map/ppermute | solution.py:38
  105.1 0.2 copy.48
  105.2 2.6 %pad_maximum_fusion.1 = f32[384,18,128]{0,1,2:T(8,128)S(1)} fusion(f32[384,1,128]{0,1,2:T(1,128)S(1)} %copy.50, f32[384,16,128]{0,1,2:T(8,128)} %copy.49, f32[384,1,128]{0,1,2:T(1,128)S(1)} %copy.48), kind=kLoop, calls=%fused_computation.12 | loop fusion | flops 1769472 | bytes 7077888 | tf_op jit(solution)/shard_map/concatenate | solution.py:40
  107.8 2.5 %collective-permute-start.14 = (f32[384,18,1]{0,1,2:T(8,128)S(1)}, f32[384,18,1]{0,1,2:T(8,128)S(1)}, u32[]{:S(2)}, u32[]{:S(2)}) collective-permute-start(f32[384,18,1]{0,1,2:T(8,128)S(1)} %get-tuple-element.59), channel_id=1, source_target_pairs={{1,0},{2,1},{3,2},{5,4},{6,5},{7,6},{9,8},{10,9},{11,10},{13,12},{... | collective-permute-start | bytes 82952 | tf_op jit(solution)/shard_map/ppermute | solution.py:39
  110.3 3.1 %collective-permute-start.13 = (f32[384,18,1]{0,1,2:T(8,128)S(1)}, f32[384,18,1]{0,1,2:T(8,128)S(1)}, u32[]{:S(2)}, u32[]{:S(2)}) collective-permute-start(f32[384,18,1]{0,1,2:T(8,128)S(1)} %get-tuple-element.58), channel_id=1, source_target_pairs={{0,1},{1,2},{2,3},{4,5},{5,6},{6,7},{8,9},{9,10},{10,11},{12,13},{... | collective-permute-start | bytes 82952 | tf_op jit(solution)/shard_map/ppermute | solution.py:38
  113.4 2.4 %copy.52 = f32[384,18,128]{0,2,1:T(8,128)} copy(f32[384,18,128]{0,1,2:T(8,128)S(1)} %pad_maximum_fusion.1) | data formatting | bytes 7077888 | tf_op jit(solution)/shard_map/concatenate | solution.py:40
  115.9 0.1 copy.45
  116.2 9.0 %fusion.8 = f32[384,16,128]{0,2,1:T(8,128)} fusion(f32[384,18,1]{0,2,1:T(1,128)S(1)} %copy.54, f32[384,18,128]{0,2,1:T(8,128)} %copy.52, f32[384,18,1]{0,2,1:T(1,128)S(1)} %copy.51, f32[384,1,128]{0,2,1:T(8,128)S(1)} %copy.47, f32[384,16,128]{0,2,1:T(8,128)} %bitcast.49, f32[384,1,128]{0,2,1:T(8,128)S(1)} %copy.45, f32[16,128]{1,0:T(8,128)S(1)} %get-tuple-element.68, ...), kind=kLoop, calls=%fused_computation.15 | loop fusion | flops 10223616 | bytes 10319872 | tf_op jit(solution)/shard_map/add | solution.py:46
  125.1 3.5 %copy.55 = f32[384,16,128]{2,1,0:T(8,128)} copy(f32[384,16,128]{0,2,1:T(8,128)} %fusion.8) | data formatting | bytes 6291456 | tf_op jit(solution)/shard_map/add | solution.py:46
  (57 shorter events, 1.5 us)
Async XLA Ops:
  0.0 42.9 %copy-start = (f32[384,384]{1,0:T(8,128)S(1)}, f32[384,384]{1,0:T(8,128)}, u32[]{:S(2)}) copy-start(f32[384,384]{1,0:T(8,128)} %param.15) | copy-start | bytes 1769476
  0.0 15.2 %copy-start.5 = (s32[512]{0:T(512)S(1)}, s32[512]{0:T(512)}, u32[]{:S(2)}) copy-start(s32[512]{0:T(512)} %param.12) | copy-start | bytes 6148
  8.2 26.9 %all-to-all-start = ((bf16[8,128,384]{2,1,0:T(8,128)(2,1)}), bf16[8,128,384]{2,1,0:T(8,128)(2,1)S(1)}, u32[]{:S(2)}, u32[]{:S(2)}) async-start(bf16[8,128,384]{2,1,0:T(8,128)(2,1)} %bitcast.6), calls=%async_computation | async-start | bytes 1572864 | tf_op jit(solution)/shard_map/all_to_all | solution.py:91
  17.7 6.3 %collective-permute-start = (s32[1,128]{1,0:T(1,128)S(1)}, s32[1,128]{1,0:T(1,128)S(1)}, u32[]{:S(2)}, u32[]{:S(2)}) collective-permute-start(s32[1,128]{1,0:T(1,128)S(1)} %get-tuple-element.76), channel_id=1, source_target_pairs={{0,4},{4,0},{8,12},{12,8},{16,20},{20,16},{24,28},{28,24},{1,5},{5... | collective-permute-start | bytes 1544 | tf_op jit(solution)/shard_map/ppermute | solution.py:22
  19.3 7.8 %collective-permute-start.1 = (s32[1,128]{1,0:T(1,128)S(1)}, s32[1,128]{1,0:T(1,128)S(1)}, u32[]{:S(2)}, u32[]{:S(2)}) collective-permute-start(s32[1,128]{1,0:T(1,128)S(1)} %get-tuple-element.75), channel_id=1, source_target_pairs={{0,8},{4,12},{8,0},{12,4},{16,24},{20,28},{24,16},{28,20},{1,9},{5... | collective-permute-start | bytes 1544 | tf_op jit(solution)/shard_map/ppermute | solution.py:22
  20.5 10.4 %collective-permute-start.2 = (s32[1,128]{1,0:T(1,128)S(1)}, s32[1,128]{1,0:T(1,128)S(1)}, u32[]{:S(2)}, u32[]{:S(2)}) collective-permute-start(s32[1,128]{1,0:T(1,128)S(1)} %get-tuple-element.74), channel_id=1, source_target_pairs={{0,12},{4,8},{8,4},{12,0},{16,28},{20,24},{24,20},{28,16},{1,13},{... | collective-permute-start | bytes 1544 | tf_op jit(solution)/shard_map/ppermute | solution.py:22
  20.5 13.2 %collective-permute-start.3 = (s32[1,128]{1,0:T(1,128)S(1)}, s32[1,128]{1,0:T(1,128)S(1)}, u32[]{:S(2)}, u32[]{:S(2)}) collective-permute-start(s32[1,128]{1,0:T(1,128)S(1)} %get-tuple-element.73), channel_id=1, source_target_pairs={{0,16},{4,20},{8,24},{12,28},{16,0},{20,4},{24,8},{28,12},{1,17},{... | collective-permute-start | bytes 1544 | tf_op jit(solution)/shard_map/ppermute | solution.py:22
  22.8 12.0 %collective-permute-start.4 = (s32[1,128]{1,0:T(1,128)S(1)}, s32[1,128]{1,0:T(1,128)S(1)}, u32[]{:S(2)}, u32[]{:S(2)}) collective-permute-start(s32[1,128]{1,0:T(1,128)S(1)} %get-tuple-element.72), channel_id=1, source_target_pairs={{0,20},{4,16},{8,28},{12,24},{16,4},{20,0},{24,12},{28,8},{1,21},{... | collective-permute-start | bytes 1544 | tf_op jit(solution)/shard_map/ppermute | solution.py:22
  24.0 10.8 %collective-permute-start.5 = (s32[1,128]{1,0:T(1,128)S(1)}, s32[1,128]{1,0:T(1,128)S(1)}, u32[]{:S(2)}, u32[]{:S(2)}) collective-permute-start(s32[1,128]{1,0:T(1,128)S(1)} %get-tuple-element.71), channel_id=1, source_target_pairs={{0,24},{4,28},{8,16},{12,20},{16,8},{20,12},{24,0},{28,4},{1,25},{... | collective-permute-start | bytes 1544 | tf_op jit(solution)/shard_map/ppermute | solution.py:22
  27.1 7.8 %collective-permute-start.6 = (s32[1,128]{1,0:T(1,128)S(1)}, s32[1,128]{1,0:T(1,128)S(1)}, u32[]{:S(2)}, u32[]{:S(2)}) collective-permute-start(s32[1,128]{1,0:T(1,128)S(1)} %get-tuple-element.70), channel_id=1, source_target_pairs={{0,28},{4,24},{8,20},{12,16},{16,12},{20,8},{24,4},{28,0},{1,29},{... | collective-permute-start | bytes 1544 | tf_op jit(solution)/shard_map/ppermute | solution.py:22
  51.3 1.7 %copy-start.1 = (f32[2048,384]{1,0:T(8,128)}, f32[2048,384]{1,0:T(8,128)S(1)}, u32[]{:S(2)}) copy-start(f32[2048,384]{1,0:T(8,128)S(1)} %fusion.34) | copy-start | bytes 9437188
  53.2 8.1 %collective-permute-start.8 = (f32[384,1,128]{2,0,1:T(8,128)S(1)}, f32[384,1,128]{2,0,1:T(8,128)S(1)}, u32[]{:S(2)}, u32[]{:S(2)}) collective-permute-start(f32[384,1,128]{2,0,1:T(8,128)S(1)} %copy.57), channel_id=1, source_target_pairs={{4,0},{8,4},{12,8},{16,12},{20,16},{24,20},{28,24},{0,28},{5,1},{9... | collective-permute-start | bytes 589832 | tf_op jit(solution)/shard_map/ppermute | solution.py:39
  55.8 7.7 %collective-permute-start.7 = (f32[384,1,128]{2,0,1:T(8,128)S(1)}, f32[384,1,128]{2,0,1:T(8,128)S(1)}, u32[]{:S(2)}, u32[]{:S(2)}) collective-permute-start(f32[384,1,128]{2,0,1:T(8,128)S(1)} %copy.56), channel_id=1, source_target_pairs={{0,4},{4,8},{8,12},{12,16},{16,20},{20,24},{24,28},{28,0},{1,5},{5... | collective-permute-start | bytes 589832 | tf_op jit(solution)/shard_map/ppermute | solution.py:38
  63.7 10.2 %copy-start.4 = (f32[4,16,128]{2,1,0:T(8,128)S(1)}, f32[4,16,128]{2,1,0:T(8,128)}, u32[]{:S(2)}) copy-start(f32[4,16,128]{2,1,0:T(8,128)} %param.17) | copy-start | bytes 98308
  66.4 10.3 %collective-permute-start.10 = (f32[384,18,1]{0,1,2:T(8,128)S(1)}, f32[384,18,1]{0,1,2:T(8,128)S(1)}, u32[]{:S(2)}, u32[]{:S(2)}) collective-permute-start(f32[384,18,1]{0,1,2:T(8,128)S(1)} %get-tuple-element.61), channel_id=1, source_target_pairs={{1,0},{2,1},{3,2},{5,4},{6,5},{7,6},{9,8},{10,9},{11,10},{13,12},{... | collective-permute-start | bytes 82952 | tf_op jit(solution)/shard_map/ppermute | solution.py:39
  70.7 6.0 %collective-permute-start.9 = (f32[384,18,1]{0,1,2:T(8,128)S(1)}, f32[384,18,1]{0,1,2:T(8,128)S(1)}, u32[]{:S(2)}, u32[]{:S(2)}) collective-permute-start(f32[384,18,1]{0,1,2:T(8,128)S(1)} %get-tuple-element.60), channel_id=1, source_target_pairs={{0,1},{1,2},{2,3},{4,5},{5,6},{6,7},{8,9},{9,10},{10,11},{12,13},{... | collective-permute-start | bytes 82952 | tf_op jit(solution)/shard_map/ppermute | solution.py:38
  74.0 2.8 %copy-start.3 = (f32[16,128]{1,0:T(8,128)S(1)}, f32[16,128]{1,0:T(8,128)}, u32[]{:S(2)}) copy-start(f32[16,128]{1,0:T(8,128)} %param.16) | copy-start | bytes 24580
  91.3 1.7 %copy-start.2 = (f32[2048,384]{1,0:T(8,128)}, f32[2048,384]{1,0:T(8,128)S(1)}, u32[]{:S(2)}) copy-start(f32[2048,384]{1,0:T(8,128)S(1)} %fusion.35) | copy-start | bytes 9437188
  93.1 7.8 %collective-permute-start.12 = (f32[384,1,128]{2,0,1:T(8,128)S(1)}, f32[384,1,128]{2,0,1:T(8,128)S(1)}, u32[]{:S(2)}, u32[]{:S(2)}) collective-permute-start(f32[384,1,128]{2,0,1:T(8,128)S(1)} %copy.59), channel_id=1, source_target_pairs={{4,0},{8,4},{12,8},{16,12},{20,16},{24,20},{28,24},{0,28},{5,1},{9... | collective-permute-start | bytes 589832 | tf_op jit(solution)/shard_map/ppermute | solution.py:39
  95.5 9.5 %collective-permute-start.11 = (f32[384,1,128]{2,0,1:T(8,128)S(1)}, f32[384,1,128]{2,0,1:T(8,128)S(1)}, u32[]{:S(2)}, u32[]{:S(2)}) collective-permute-start(f32[384,1,128]{2,0,1:T(8,128)S(1)} %copy.58), channel_id=1, source_target_pairs={{0,4},{4,8},{8,12},{12,16},{16,20},{20,24},{24,28},{28,0},{1,5},{5... | collective-permute-start | bytes 589832 | tf_op jit(solution)/shard_map/ppermute | solution.py:38
  107.8 8.2 %collective-permute-start.14 = (f32[384,18,1]{0,1,2:T(8,128)S(1)}, f32[384,18,1]{0,1,2:T(8,128)S(1)}, u32[]{:S(2)}, u32[]{:S(2)}) collective-permute-start(f32[384,18,1]{0,1,2:T(8,128)S(1)} %get-tuple-element.59), channel_id=1, source_target_pairs={{1,0},{2,1},{3,2},{5,4},{6,5},{7,6},{9,8},{10,9},{11,10},{13,12},{... | collective-permute-start | bytes 82952 | tf_op jit(solution)/shard_map/ppermute | solution.py:39
  110.3 5.8 %collective-permute-start.13 = (f32[384,18,1]{0,1,2:T(8,128)S(1)}, f32[384,18,1]{0,1,2:T(8,128)S(1)}, u32[]{:S(2)}, u32[]{:S(2)}) collective-permute-start(f32[384,18,1]{0,1,2:T(8,128)S(1)} %get-tuple-element.58), channel_id=1, source_target_pairs={{0,1},{1,2},{2,3},{4,5},{5,6},{6,7},{8,9},{9,10},{10,11},{12,13},{... | collective-permute-start | bytes 82952 | tf_op jit(solution)/shard_map/ppermute | solution.py:38
